TPU v7x, 32 devices: a whole 2x2x4 slice. The times are simulated.
32 devices in a mesh: group: 4 (over z), dp: 2 (over y), mp: 4 (over x, core).
Axes of the slice: x: 2, y: 2, z: 4, core: 2. Of those that a mesh axis runs over, the one named last changes fastest.
Arguments:
- image_feats: bfloat16 [48, 1280], P(('group', 'dp')), may hold values from -6 to 6
- image_proj: bfloat16 [1280, 1024], P(None, 'mp'), may hold values from -0.15625 to 0.15625
- tokens: bfloat16 [3, 16, 196, 768], P(None, ('group', 'dp')), may hold values from -6 to 6
- counts: int32 [3, 16], P(None, ('group', 'dp')), may hold values from 50 to 196
- pairing: int32 [3, 16], P(None, ('group', 'dp')), may hold values from 0 to 47, as said below
- w_up: bfloat16 [3, 768, 3072], P(None, None, 'mp'), may hold values from -0.21875 to 0.21875
- w_down: bfloat16 [3, 768, 3072], P(None, None, 'mp'), may hold values from -0.109375 to 0.109375
- w_proj: bfloat16 [3, 768, 1024], P(None, None, 'mp'), may hold values from -0.21875 to 0.21875
Outputs:
- grad_up: float32 [3, 768, 3072], P(None, ('group', 'dp'), 'mp')
- grad_down: float32 [3, 768, 3072], P(None, ('group', 'dp'), 'mp')
- grad_proj: float32 [3, 768, 1024], P(None, ('group', 'dp'), 'mp')
Inputs may be any that keep to these rules, and one draw needn't show every extreme that they name: `pairing`: each of the 48 anchors is paired with exactly one sample of one modality.
All inputs are finite; a program needn't handle non-finite values.
Results may differ from a plain program's by a relative error of at most 0.017.
Values may be sent and summed in bfloat16 or wider, within the bound.
A program may use at most 128 MiB of HBM per device.

v0:
```python
import jax
import jax.numpy as jnp
from jax import lax
from jax.sharding import PartitionSpec as P

inverse_temp = 14.285714285714286
norm_eps = 1e-05
unit_eps = 1e-06
root_half = 0.7071067811865476
gauss_coef = 0.3989422804014327


def normalize_rows(values):
    centre = jnp.mean(values, axis=-1, keepdims=True)
    spread = jnp.mean(jnp.square(values - centre), axis=-1, keepdims=True)
    scale_inv = lax.rsqrt(spread + norm_eps)
    return ((values - centre) * scale_inv, scale_inv)


def gelu_value(values):
    return 0.5 * values * (1.0 + lax.erf(values * root_half))


def gelu_slope(values):
    return (
        0.5 * (1.0 + lax.erf(values * root_half))
        + values * jnp.exp(-0.5 * values * values) * gauss_coef
    )


def body(image_feats, image_proj, tokens, counts, pairing, w_up, w_down, w_proj):
    image_normed = normalize_rows(image_feats.astype(jnp.float32))[0].astype(jnp.bfloat16)
    embed_cols = jnp.dot(image_normed, image_proj, preferred_element_type=jnp.float32)
    anchor_sq = lax.psum(jnp.sum(embed_cols * embed_cols, axis=-1), "mp")
    anchor_cols = (embed_cols * lax.rsqrt(anchor_sq + unit_eps)[:, None]).astype(jnp.bfloat16)
    num_samples = tokens.shape[1]
    num_patches = tokens.shape[2]
    feature_width = tokens.shape[3]
    positions = jnp.arange(num_patches, dtype=jnp.int32)
    inside = positions[None, None, :] < counts[:, :, None]
    weight = jnp.where(inside, 1.0 / counts[:, :, None].astype(jnp.float32), 0.0)
    mask_bf = inside.astype(jnp.bfloat16)
    normed_list = []
    pre_list = []
    pool_list = []
    partials = []
    for modality in range(3):
        normed = (
            normalize_rows(tokens[modality].astype(jnp.float32))[0]
            .astype(jnp.bfloat16)
            .reshape(-1, feature_width)
        )
        pre_act = jnp.dot(normed, w_up[modality], preferred_element_type=jnp.float32).reshape(
            num_samples, num_patches, -1
        )
        act_pool = jnp.einsum("sp,spf->sf", weight[modality], gelu_value(pre_act)).astype(
            jnp.bfloat16
        )
        partials.append(
            lax.dot_general(
                act_pool,
                w_down[modality],
                (((1,), (1,)), ((), ())),
                preferred_element_type=jnp.float32,
            )
        )
        normed_list.append(normed)
        pre_list.append(pre_act)
        pool_list.append(act_pool)
    token_pool = jnp.einsum(
        "msp,mspd->msd", mask_bf, tokens, preferred_element_type=jnp.float32
    ) / counts[:, :, None].astype(jnp.float32)
    pooled = token_pool + lax.psum(jnp.stack(partials), "mp")
    feat_norm, scale_inv = normalize_rows(pooled)
    feat = feat_norm.astype(jnp.bfloat16)
    embedded = jnp.einsum("msd,mde->mse", feat, w_proj, preferred_element_type=jnp.float32)
    embed_sq = lax.psum(jnp.sum(embedded * embedded, axis=-1), "mp")
    inv_norm = lax.rsqrt(embed_sq + unit_eps)[..., None]
    unit_rows = embedded * inv_norm
    queries = unit_rows.astype(jnp.bfloat16).reshape(3 * num_samples, -1)
    target_rows = pairing.reshape(-1)
    own_table = lax.all_gather(anchor_cols, ("group", "dp"), axis=0, tiled=True)
    part_logits = jnp.dot(queries, own_table.T, preferred_element_type=jnp.float32)
    logits = inverse_temp * lax.psum(part_logits, "mp")
    exp_logits = jnp.exp(logits)
    prob_bf = (exp_logits / jnp.sum(exp_logits, axis=-1, keepdims=True)).astype(jnp.bfloat16)
    weighted = jnp.dot(prob_bf, own_table, preferred_element_type=jnp.float32)
    target = jnp.take(own_table, target_rows, axis=0).astype(jnp.float32)
    d_unit = (inverse_temp * (weighted - target)).reshape(unit_rows.shape)
    unit_dots = lax.psum(jnp.sum(unit_rows * d_unit, axis=-1), "mp")
    d_embed = ((d_unit - unit_rows * unit_dots[..., None]) * inv_norm).astype(jnp.bfloat16)
    d_feat = lax.psum(
        jnp.einsum("mse,mde->msd", d_embed, w_proj, preferred_element_type=jnp.float32), "mp"
    )
    d_pooled = (
        scale_inv
        * (
            d_feat
            - jnp.mean(d_feat, axis=-1, keepdims=True)
            - feat_norm * jnp.mean(d_feat * feat_norm, axis=-1, keepdims=True)
        )
    ).astype(jnp.bfloat16)
    pool_stack = jnp.stack(pool_list)
    feat_all, dpool_all, act_all, dembed_all = (
        lax.all_gather(feat, ("group", "dp"), axis=1, tiled=True),
        lax.all_gather(d_pooled, ("group", "dp"), axis=1, tiled=True),
        lax.all_gather(pool_stack, ("group", "dp"), axis=1, tiled=True),
        lax.all_gather(d_embed, ("group", "dp"), axis=1, tiled=True),
    )
    row_count = feature_width // lax.axis_size(("group", "dp"))
    row_start = lax.axis_index(("group", "dp")) * row_count
    feat_rows = lax.dynamic_slice_in_dim(feat_all, row_start, row_count, 2)
    dpool_rows = lax.dynamic_slice_in_dim(dpool_all, row_start, row_count, 2)
    down_shards = jnp.einsum(
        "msd,msf->mdf", dpool_rows, act_all, preferred_element_type=jnp.float32
    )
    proj_shards = jnp.einsum(
        "msd,mse->mde", feat_rows, dembed_all, preferred_element_type=jnp.float32
    )
    joined_list = []
    for modality in range(3):
        d_act = jnp.dot(d_pooled[modality], w_down[modality], preferred_element_type=jnp.float32)
        d_pre = (
            weight[modality][:, :, None] * d_act[:, None, :] * gelu_slope(pre_list[modality])
        ).astype(jnp.bfloat16)
        grad_up = lax.dot_general(
            normed_list[modality],
            d_pre.reshape(-1, d_pre.shape[2]),
            (((0,), (0,)), ((), ())),
            preferred_element_type=jnp.float32,
        )
        joined_list.append(grad_up)
    stacked = jnp.stack(joined_list)
    stacked = lax.psum_scatter(stacked, ("group", "dp"), scatter_dimension=1, tiled=True)
    return (stacked, down_shards, proj_shards)


def solution(mesh):
    in_specs = (
        P(("group", "dp"), None),
        P(None, "mp"),
        P(None, ("group", "dp"), None, None),
        P(None, ("group", "dp")),
        P(None, ("group", "dp")),
        P(None, None, "mp"),
        P(None, None, "mp"),
        P(None, None, "mp"),
    )
    out_specs = (
        P(None, ("group", "dp"), "mp"),
        P(None, ("group", "dp"), "mp"),
        P(None, ("group", "dp"), "mp"),
    )
    return jax.shard_map(body, mesh=mesh, in_specs=in_specs, out_specs=out_specs, check_vma=False)
```

profile of v0, /device:TPU:0, one launch (start us, length us, event | category | flops | bytes accessed | tf_op | source)
XLA Modules:
  0.0 264.3 jit_solution(3255284426985158077)
XLA Ops:
  7.2 0.9 copy.51
  8.1 0.7 broadcast_divide_fusion
  8.8 0.7 convert_element_type.135
  9.4 0.8 copy.57
  10.4 3.0 %convert_reduce_fusion.2 = (f32[2,196]{0,1:T(8,128)S(1)}, f32[2,196]{0,1:T(8,128)S(1)}, f32[2,196]{0,1:T(8,128)S(1)}) fusion(bf16[3,2,196,768]{3,1,2,0:T(2,128)(2,1)} %param.10), kind=kLoop, calls=%fused_computation.14 | loop fusion | flops 1805160 | bytes 1811040 | tf_op jit(solution)/shard_map/reduce_sum | solution.py:14
  13.5 5.6 %fusion.32 = (f32[2,196]{0,1:T(8,128)S(1)}, f32[2,196]{0,1:T(8,128)S(1)}, f32[2,196]{0,1:T(8,128)S(1)}) fusion(f32[2,196]{0,1:T(8,128)S(1)} %broadcast_multiply_fusion.2, bf16[3,2,196,768]{3,1,2,0:T(2,128)(2,1)S(1)} %copy-done.1, f32[2,196]{0,1:T(8,128)S(1)} %get-tuple-element.32, f32[2,196]{0,1:T(8,128)S(1)} %get-tuple-element.31), kind=kLoop, calls=%fused_computation.52 | loop fusion | flops 3611496 | bytes 1815744 | tf_op jit(solution)/shard_map/reduce_sum | solution.py:15
  19.2 3.2 %fusion.116 = (bf16[2,196,768]{2,0,1:T(2,128)(2,1)}, bf16[2,196,768]{2,0,1:T(2,128)(2,1)}, bf16[2,196,768]{2,0,1:T(2,128)(2,1)}) fusion(f32[2,196]{0,1:T(8,128)S(1)} %add_rsqrt_fusion.2, f32[2,196]{0,1:T(8,128)S(1)} %broadcast_multiply_fusion.2, bf16[3,2,196,768]{3,1,2,0:T(2,128)(2,1)S(1)} %copy-done.1, f32[2,196]{0,1:T(8,128)S(1)} %add_rsqrt_fusion.1, ...), kind=kLoop, calls=%fused_computation.128 | loop fusion | flops 3612672 | bytes 3622080 | tf_op jit(solution)/shard_map/convert_element_type | solution.py:50
  22.4 3.2 %fusion.33 = (bf16[2,196,768]{2,0,1:T(2,128)(2,1)}, bf16[2,196,768]{2,0,1:T(2,128)(2,1)}, bf16[2,196,768]{2,0,1:T(2,128)(2,1)}) fusion(f32[2,196]{0,1:T(8,128)S(1)} %add_rsqrt_fusion.2, f32[2,196]{0,1:T(8,128)S(1)} %broadcast_multiply_fusion.2, bf16[3,2,196,768]{3,1,2,0:T(2,128)(2,1)S(1)} %copy-done.1, f32[2,196]{0,1:T(8,128)S(1)} %add_rsqrt_fusion.1, ...), kind=kLoop, calls=%fused_computation.53 | loop fusion | flops 3612672 | bytes 3622080 | tf_op jit(solution)/shard_map/convert_element_type | solution.py:50
  25.9 2.2 fusion.66
  28.1 2.4 fusion.60
  32.6 1.9 fusion.54
  35.6 12.8 %psum.42 = f32[3,2,768]{2,1,0:T(2,128)S(1)} all-reduce(f32[3,2,768]{2,1,0:T(2,128)S(1)} %pad_maximum_fusion.1), channel_id=1, replica_groups=mesh['group'=4,'dp'=2,'mp'=4] {'mp'}, use_global_device_ids=true, to_apply=%region_6.7 | all-reduce | flops 4608 | bytes 36864 | tf_op jit(solution)/shard_map/psum | solution.py:73
  50.4 5.8 %all-reduce = (f32[6]{0:T(128)S(1)}, f32[3,2]{1,0:T(4,128)S(1)}) all-reduce(f32[6]{0:T(128)S(1)} %get-tuple-element.27, f32[3,2]{1,0:T(4,128)S(1)} %get-tuple-element.29), channel_id=1, replica_groups=mesh['group'=4,'dp'=2,'mp'=4] {'mp'}, use_global_device_ids=true, to_apply=%region_14.15 | all-reduce | flops 12 | bytes 96 | tf_op jit(solution)/shard_map/psum | solution.py:34
  56.4 30.8 %all-gather = bf16[8,6,256]{2,1,0:T(8,128)(2,1)S(1)} all-gather(bf16[1,6,256]{2,1,0:T(8,128)(2,1)S(1)} %fusion.134), channel_id=1, replica_groups=mesh['group'=4,'dp'=2,'mp'=4] {'group','dp'}, dimensions={0}, use_global_device_ids=true | all-gather | bytes 27648 | tf_op jit(solution)/shard_map/all_gather | solution.py:82
  87.3 5.7 %psum.45 = f32[6,48]{1,0:T(8,128)S(1)} all-reduce(f32[6,48]{1,0:T(8,128)S(1)} %fusion.161), channel_id=1, replica_groups=mesh['group'=4,'dp'=2,'mp'=4] {'mp'}, use_global_device_ids=true, to_apply=%region_15.16 | all-reduce | flops 288 | bytes 2304 | tf_op jit(solution)/shard_map/psum | solution.py:84
  93.2 0.6 gather_fusion
  94.2 5.7 %psum.46 = f32[3,2]{1,0:T(4,128)S(1)} all-reduce(f32[3,2]{1,0:T(4,128)S(1)} %multiply_reduce_fusion.3), channel_id=1, replica_groups=mesh['group'=4,'dp'=2,'mp'=4] {'mp'}, use_global_device_ids=true, to_apply=%region_18.19 | all-reduce | flops 6 | bytes 48 | tf_op jit(solution)/shard_map/psum | solution.py:90
  100.4 10.5 %psum.47 = f32[3,2,768]{2,1,0:T(2,128)S(1)} all-reduce(f32[3,2,768]{2,1,0:T(2,128)S(1)} %fusion.162), channel_id=1, replica_groups=mesh['group'=4,'dp'=2,'mp'=4] {'mp'}, use_global_device_ids=true, to_apply=%region_19.20 | all-reduce | flops 4608 | bytes 36864 | tf_op jit(solution)/shard_map/psum | solution.py:92
  111.2 1.5 fusion.62
  112.7 1.7 fusion.56
  114.4 1.6 fusion.50
  116.0 1.1 convolution_bitcast_fusion.2
  117.4 1.1 convolution_bitcast_fusion.1
  118.9 1.1 convolution_bitcast_fusion
  120.0 3.4 %pad_maximum_fusion = f32[3,768,768]{2,1,0:T(8,128)} fusion(f32[1,768,768]{2,1,0:T(8,128)S(1)} %convolution_bitcast_fusion, f32[1,768,768]{2,1,0:T(8,128)S(1)} %convolution_bitcast_fusion.1, f32[1,768,768]{2,1,0:T(8,128)S(1)} %convolution_bitcast_fusion.2), kind=kLoop, calls=%fused_computation.1 | loop fusion | flops 3538944 | bytes 14155776 | tf_op jit(solution)/shard_map/stack | solution.py:133
  123.5 31.4 %all_gather.19 = bf16[3,16,256]{2,0,1:T(4,128)(2,1)S(1)} all-gather(bf16[3,2,256]{2,0,1:T(4,128)(2,1)S(1)} %copy.68), channel_id=1, replica_groups=mesh['group'=4,'dp'=2,'mp'=4] {'group','dp'}, dimensions={1}, use_global_device_ids=true | all-gather | bytes 27648 | tf_op jit(solution)/shard_map/all_gather | solution.py:108
  154.9 32.1 %all_gather.17 = bf16[3,16,768]{2,0,1:T(4,128)(2,1)S(1)} all-gather(bf16[3,2,768]{2,0,1:T(4,128)(2,1)S(1)} %copy.64), channel_id=1, replica_groups=mesh['group'=4,'dp'=2,'mp'=4] {'group','dp'}, dimensions={1}, use_global_device_ids=true | all-gather | bytes 82944 | tf_op jit(solution)/shard_map/all_gather | solution.py:107
  187.0 31.0 %all_gather.16 = bf16[3,16,768]{2,0,1:T(4,128)(2,1)S(1)} all-gather(bf16[3,2,768]{2,0,1:T(4,128)(2,1)S(1)} %copy.62), channel_id=1, replica_groups=mesh['group'=4,'dp'=2,'mp'=4] {'group','dp'}, dimensions={1}, use_global_device_ids=true | all-gather | bytes 82944 | tf_op jit(solution)/shard_map/all_gather | solution.py:106
  218.0 32.0 %all_gather.18 = bf16[3,16,768]{2,0,1:T(4,128)(2,1)S(1)} all-gather(bf16[3,2,768]{2,0,1:T(4,128)(2,1)S(1)} %copy.66), channel_id=1, replica_groups=mesh['group'=4,'dp'=2,'mp'=4] {'group','dp'}, dimensions={1}, use_global_device_ids=true | all-gather | bytes 82944 | tf_op jit(solution)/shard_map/all_gather | solution.py:105
  250.2 1.0 fusion.123
  251.2 1.2 fusion.117
  252.4 5.0 %reduce-scatter.2.cloned.1.call-done = f32[3,96,768]{2,1,0:T(8,128)} async-done(((f32[3,768,768]{2,1,0:T(8,128)}), f32[3,96,768]{2,1,0:T(8,128)}) %reduce-scatter.2.cloned.1.call-update) | async-done | bytes 884752 | tf_op jit(solution)/shard_map/reduce_scatter | solution.py:134
  (96 shorter events, 8.3 us)
Async XLA Ops:
  7.2 42.5 %copy-start = (bf16[3,768,256]{2,1,0:T(8,128)(2,1)S(1)}, bf16[3,768,256]{2,1,0:T(8,128)(2,1)}, u32[]{:S(2)}) copy-start(bf16[3,768,256]{2,1,0:T(8,128)(2,1)} %param.15) | copy-start | bytes 3538948
  7.2 250.3 %reduce-scatter.2.cloned.1.call-start = ((), (), s32[]{:S(2)}) async-start(), calls=%async_computation.1 | async-start | bytes 7962624 | tf_op jit(solution)/shard_map/reduce_scatter | solution.py:134
  10.4 3.1 %copy-start.1 = (bf16[3,2,196,768]{3,1,2,0:T(2,128)(2,1)S(1)}, bf16[3,2,196,768]{3,1,2,0:T(2,128)(2,1)}, u32[]{:S(2)}) copy-start(bf16[3,2,196,768]{3,1,2,0:T(2,128)(2,1)} %param.10) | copy-start | bytes 5419012
  25.9 2.2 copy-start.7
  28.1 2.4 copy-start.14
  28.1 2.8 %copy-start.2 = (bf16[3,768,768]{2,1,0:T(8,128)(2,1)S(1)}, bf16[3,768,768]{2,1,0:T(8,128)(2,1)}, u32[]{:S(2)}) copy-start(bf16[3,768,768]{2,1,0:T(8,128)(2,1)} %param.14) | copy-start | bytes 10616836
  30.5 1.1 copy-start.10
  31.6 1.1 copy-start.6
  34.5 1.0 copy-start.12
  35.6 13.8 %copy-start.8 = (bf16[6,1280]{1,0:T(8,128)(2,1)S(1)}, bf16[6,1280]{1,0:T(8,128)(2,1)}, u32[]{:S(2)}) copy-start(bf16[6,1280]{1,0:T(8,128)(2,1)} %param.8) | copy-start | bytes 46084
  48.8 1.3 copy-start.9
  112.7 3.2 %copy-start.5 = (bf16[2,196,768]{2,0,1:T(2,128)(2,1)S(1)}, bf16[2,196,768]{2,0,1:T(2,128)(2,1)}, u32[]{:S(2)}) copy-start(bf16[2,196,768]{2,0,1:T(2,128)(2,1)} %get-tuple-element.15) | copy-start | bytes 1806340
  112.7 3.2 %copy-start.15 = (f32[2,196,768]{2,1,0:T(8,128)S(1)}, f32[2,196,768]{2,1,0:T(8,128)}, u32[]{:S(2)}) copy-start(f32[2,196,768]{2,1,0:T(8,128)} %copy-done.14) | copy-start | bytes 3612676
  115.9 1.1 copy-start.4
  116.0 1.5 copy-start.11
  117.4 1.1 copy-start.3
  117.4 1.5 copy-start.13
Sparse Core Ops, SparseCore 0:
  123.5 133.8 reduce-scatter.1
where the time goes:
time: 265 us; the launch traced here: 264 us
  blocking collectives  198 us (75%)
  other arithmetic  21.7 us (8%)
  matrix products  20.9 us (8%)
  between operations  14.4 us (5%)
  waiting for transfers between devices  5.06 us (2%)
  local copies, waits for them, and re-layouts  4.4 us (2%)
    all_gather x1, blocking collectives, body(): lax.all_gather(pool_stack, ('group', 'dp'), axis=1, tiled=True)  32.1 us
    all_gather x1, blocking collectives, body(): lax.all_gather(feat, ('group', 'dp'), axis=1, tiled=True)  32 us
    all_gather x1, blocking collectives, body(): lax.all_gather(d_embed, ('group', 'dp'), axis=1, tiled=True)  31.4 us
    all_gather x1, blocking collectives, body(): lax.all_gather(d_pooled, ('group', 'dp'), axis=1, tiled=True)  31 us
    all_gather x1, blocking collectives, body(): own_table = lax.all_gather(anchor_cols, ('group', 'dp'), axis=0, tiled=True)  30.8 us
    psum x1, blocking collectives, body(): pooled = token_pool + lax.psum(jnp.stack(partials), 'mp')  12.8 us
    psum x1, blocking collectives, body(): lax.psum(jnp.einsum('mse,mde->msd', d_embed, w_proj, preferred_element_ty...  10.5 us
    dot_general x3, matrix products, body(): jnp.dot(normed, w_up[modality], preferred_element_type=jnp.float32)  6.47 us
  transfers between devices with their start and end apart: 1, of which 1 were waited for; matrix products, arithmetic and copies ran while one was open for 1% of the time, Pallas kernels for 0%

commit v1 on v0

--- a/solution.py
+++ b/solution.py
@@ -1,8 +1,13 @@
+import functools
+
 import jax
 import jax.numpy as jnp
 from jax import lax
+from jax.experimental import pallas as pl
+from jax.experimental.pallas import tpu as pltpu
 from jax.sharding import PartitionSpec as P
 
+MESH = pl.DeviceIdType.MESH
 inverse_temp = 14.285714285714286
 norm_eps = 1e-05
 unit_eps = 1e-06
@@ -28,7 +33,7 @@
     )
 
 
-def body(image_feats, image_proj, tokens, counts, pairing, w_up, w_down, w_proj):
+def plain_body(image_feats, image_proj, tokens, counts, pairing, w_up, w_down, w_proj):
     image_normed = normalize_rows(image_feats.astype(jnp.float32))[0].astype(jnp.bfloat16)
     embed_cols = jnp.dot(image_normed, image_proj, preferred_element_type=jnp.float32)
     anchor_sq = lax.psum(jnp.sum(embed_cols * embed_cols, axis=-1), "mp")
@@ -134,6 +139,325 @@
     stacked = lax.psum_scatter(stacked, ("group", "dp"), scatter_dimension=1, tiled=True)
     return (stacked, down_shards, proj_shards)
 
+def fwd_kernel(counts_ref, tok_ref, up_ref, h_ref, act_ref, pool_ref):
+    m, s = pl.program_id(0), pl.program_id(1)
+    per = pl.num_programs(1)
+    row = m * per + s
+
+    @pl.when(row == 0)
+    def _():
+        act_ref[...] = jnp.zeros_like(act_ref)
+        pool_ref[...] = jnp.zeros_like(pool_ref)
+
+    count = counts_ref[m, s]
+    x = tok_ref[0, 0].astype(jnp.float32)
+    normed = normalize_rows(x)[0].astype(jnp.bfloat16)
+    inv = 1.0 / jnp.full((x.shape[0], 1), count, jnp.int32).astype(jnp.float32)
+    index = lax.broadcasted_iota(jnp.int32, (x.shape[0], 1), 0)
+    weight = jnp.where(index < count, inv, 0.0)
+    pre = jnp.dot(normed, up_ref[0], preferred_element_type=jnp.float32)
+    phi = 0.5 * (1.0 + lax.erf(pre * root_half))
+    slope = phi + pre * jnp.exp(-0.5 * pre * pre) * gauss_coef
+    act_ref[pl.ds(row, 1), :] = jnp.sum(weight * (pre * phi), axis=0, keepdims=True)
+    pool_ref[pl.ds(row, 1), :] = jnp.sum(weight * x, axis=0, keepdims=True)
+    sloped = (weight * slope).astype(jnp.bfloat16)
+    h_ref[0] = lax.dot_general(
+        normed, sloped, (((0,), (0,)), ((), ())), preferred_element_type=jnp.float32
+    ).astype(jnp.bfloat16)
+
+
+def peer_of(r, ndp):
+    return {"group": r // ndp, "dp": lax.rem(r, ndp)}
+
+
+def mid_kernel(
+    sizes, pair_ref, img_ref, iproj_ref, act_ref, pool_ref, down_ref, proj_ref,
+    dact_ref, gdown_ref, gproj_ref,
+    e_slots, sq_slots, p_slots, l_slots, f_slots, ga, gb, gt,
+    e_ss, e_rs, sq_ss, sq_rs, p_ss, p_rs, l_ss, l_rs, f_ss, f_rs, a_ss, a_rs, b_ss, b_rs,
+):
+    ngroup, ndp, nmp, per, apd = sizes
+    nr = ngroup * ndp
+    r = lax.axis_index("group") * ndp + lax.axis_index("dp")
+    me = lax.axis_index("mp")
+    nmod = down_ref.shape[0]
+    rows = act_ref.shape[0]
+    barrier = pltpu.get_barrier_semaphore()
+    for k in range(1, nmp):
+        pl.semaphore_signal(barrier, inc=1, device_id={"mp": lax.rem(me + k, nmp)}, device_id_type=MESH)
+    for k in range(1, nr):
+        pl.semaphore_signal(barrier, inc=1, device_id=peer_of(lax.rem(r + k, nr), ndp), device_id_type=MESH)
+    pl.semaphore_wait(barrier, nmp - 1 + nr - 1)
+
+    def spread(slots, ss, rs, across_mp):
+        slot = me if across_mp else r
+        out = []
+        for k in range(1, nmp if across_mp else nr):
+            device = {"mp": lax.rem(me + k, nmp)} if across_mp else peer_of(lax.rem(r + k, nr), ndp)
+            copy = pltpu.make_async_remote_copy(
+                src_ref=slots.at[slot], dst_ref=slots.at[slot],
+                send_sem=ss.at[k - 1], recv_sem=rs.at[k - 1],
+                device_id=device, device_id_type=MESH,
+            )
+            copy.start()
+            out.append(copy)
+        return out
+
+    def arrive(copies):
+        for copy in copies:
+            copy.wait_recv()
+
+    started = []
+    row_id = lax.broadcasted_iota(jnp.int32, (rows, 1), 0)
+    of_mod = [(row_id >= m * per) & (row_id < (m + 1) * per) for m in range(nmod)]
+
+    def by_mod(values, w_ref, dim):
+        total = None
+        for m in range(nmod):
+            part = lax.dot_general(
+                jnp.where(of_mod[m], values, 0.0).astype(jnp.bfloat16), w_ref[m],
+                (((1,), (dim,)), ((), ())), preferred_element_type=jnp.float32,
+            )
+            total = part if total is None else total + part
+        return total
+
+    act = act_ref[...].astype(jnp.bfloat16).astype(jnp.float32)
+    p_slots[me] = by_mod(act, down_ref, 1)
+    pooled_copies = spread(p_slots, p_ss, p_rs, True)
+    image = normalize_rows(img_ref[...].astype(jnp.float32))[0].astype(jnp.bfloat16)
+    e_slots[r] = jnp.dot(image, iproj_ref[...], preferred_element_type=jnp.float32)
+    e_copies = spread(e_slots, e_ss, e_rs, False)
+    arrive(e_copies)
+    embed = e_slots[...].reshape(nr * 8, -1)
+    square = jnp.sum(embed * embed, axis=-1, keepdims=True)
+    sq_slots[me] = jnp.broadcast_to(square, sq_slots.shape[1:])
+    sq_copies = spread(sq_slots, sq_ss, sq_rs, True)
+
+    arrive(pooled_copies)
+    pooled = pool_ref[...]
+    for k in range(nmp):
+        pooled = pooled + p_slots[k]
+    feat_norm, scale_inv = normalize_rows(pooled)
+    ga[r] = jnp.concatenate([act, feat_norm], axis=0).astype(jnp.bfloat16)
+    a_copies = spread(ga, a_ss, a_rs, False)
+    embedded = by_mod(feat_norm, proj_ref, 0)
+    own_sq = jnp.sum(embedded * embedded, axis=-1, keepdims=True)
+
+    arrive(sq_copies)
+    square = sq_slots[0]
+    for k in range(1, nmp):
+        square = square + sq_slots[k]
+    anchors = (embed * lax.rsqrt(square[:, :1] + unit_eps)).astype(jnp.bfloat16)
+    table = jnp.concatenate([anchors, jnp.zeros((128 - nr * 8, anchors.shape[1]), jnp.bfloat16)], axis=0)
+    part = lax.dot_general(
+        embedded.astype(jnp.bfloat16), table, (((1,), (1,)), ((), ())),
+        preferred_element_type=jnp.float32,
+    )
+    col = lax.broadcasted_iota(jnp.int32, (rows, 128), 1)
+    l_slots[me] = jnp.where(col < nr * 8, part, own_sq)
+    l_copies = spread(l_slots, l_ss, l_rs, True)
+    hot = jnp.zeros((rows, 128), jnp.float32)
+    anchor_of = (col // 8) * apd + col % 8
+    valid = (col % 8 < apd) & (col < nr * 8)
+    for m in range(nmod):
+        for s in range(per):
+            hit = valid & (anchor_of == pair_ref[m, s]) & (row_id == m * per + s)
+            hot = jnp.where(hit, 1.0, hot)
+    arrive(l_copies)
+    both = l_slots[0]
+    for k in range(1, nmp):
+        both = both + l_slots[k]
+    inv_norm = lax.rsqrt(both[:, 127:] + unit_eps)
+    logits = inverse_temp * (both * inv_norm)
+    expl = jnp.where(valid, jnp.exp(jnp.where(valid, logits, 0.0)), 0.0)
+    prob = (expl / jnp.sum(expl, axis=-1, keepdims=True)).astype(jnp.bfloat16)
+    dots = jnp.sum(
+        jnp.where(valid, (prob.astype(jnp.float32) - hot) * logits, 0.0), axis=-1, keepdims=True
+    )
+    weighted = jnp.dot(prob, table, preferred_element_type=jnp.float32)
+    target = jnp.dot(hot.astype(jnp.bfloat16), table, preferred_element_type=jnp.float32)
+    d_unit = inverse_temp * (weighted - target)
+    d_embed = ((d_unit - embedded * inv_norm * dots) * inv_norm).astype(jnp.bfloat16).astype(jnp.float32)
+    f_slots[me] = by_mod(d_embed, proj_ref, 1)
+    f_copies = spread(f_slots, f_ss, f_rs, True)
+    arrive(f_copies)
+    d_feat = f_slots[0]
+    for k in range(1, nmp):
+        d_feat = d_feat + f_slots[k]
+    d_pooled = scale_inv * (
+        d_feat
+        - jnp.mean(d_feat, axis=-1, keepdims=True)
+        - feat_norm * jnp.mean(d_feat * feat_norm, axis=-1, keepdims=True)
+    )
+    wide = jnp.concatenate([d_embed, jnp.zeros((rows, ga.shape[2] - d_embed.shape[1]), jnp.float32)], axis=1)
+    gb[r] = jnp.concatenate([d_pooled, wide], axis=0).astype(jnp.bfloat16)
+    b_copies = spread(gb, b_ss, b_rs, False)
+    dact_ref[...] = by_mod(d_pooled, down_ref, 0)
+    arrive(a_copies)
+    arrive(b_copies)
+
+    all_a = ga[...].reshape(nr * 16, -1)
+    all_b = gb[...].reshape(nr * 16, -1)
+    height = gdown_ref.shape[1]
+    mine = pl.ds(pl.multiple_of(r * height, height), height)
+    lane = lax.broadcasted_iota(jnp.int32, (1, nr * 16), 1) % 16
+    width = gproj_ref.shape[2]
+    gt[...] = all_b.astype(jnp.float32).T
+    lhs = gt[mine, :]
+    for m in range(nmod):
+        keep = (lane >= m * per) & (lane < (m + 1) * per)
+        gdown_ref[m] = jnp.dot(
+            jnp.where(keep, lhs, 0.0).astype(jnp.bfloat16), all_a, preferred_element_type=jnp.float32
+        )
+    gt[...] = all_a.astype(jnp.float32).T
+    lhs = gt[mine, :]
+    for m in range(nmod):
+        keep = (lane >= 8 + m * per) & (lane < 8 + (m + 1) * per)
+        gproj_ref[m] = jnp.dot(
+            jnp.where(keep, lhs, 0.0).astype(jnp.bfloat16), all_b[:, :width],
+            preferred_element_type=jnp.float32,
+        )
+    for copy in pooled_copies + e_copies + sq_copies + a_copies + l_copies + f_copies + b_copies:
+        copy.wait_send()
+
+
+def scatter_kernel(
+    sizes, h_ref, dact_ref, out_ref, y_send, y_recv, z_send, z_recv, y_ss, y_rs, z_ss, z_rs
+):
+    ngroup, ndp, nmp, per, apd = sizes
+    g, d = lax.axis_index("group"), lax.axis_index("dp")
+    nmod, height = out_ref.shape[:2]
+    barrier = pltpu.get_barrier_semaphore()
+    pl.semaphore_signal(barrier, inc=1, device_id={"dp": 1 - d}, device_id_type=MESH)
+    for k in range(1, ngroup):
+        pl.semaphore_signal(barrier, inc=1, device_id={"group": lax.rem(g + k, ngroup)}, device_id_type=MESH)
+    pl.semaphore_wait(barrier, ngroup)
+
+    def term(m, group, dp):
+        at = pl.ds(pl.multiple_of((group * ndp + dp) * height, height), height)
+        total = None
+        for s in range(per):
+            row = m * per + s
+            part = h_ref[row, at, :].astype(jnp.float32) * dact_ref[row : row + 1, :]
+            total = part if total is None else total + part
+        return total
+
+    y_copies, z_copies = [], []
+    for m in range(nmod):
+        for group in range(ngroup):
+            y_send[m, group] = term(m, group, 1 - d).astype(jnp.bfloat16)
+        copy = pltpu.make_async_remote_copy(
+            src_ref=y_send.at[m], dst_ref=y_recv.at[m], send_sem=y_ss.at[m], recv_sem=y_rs.at[m],
+            device_id={"dp": 1 - d}, device_id_type=MESH,
+        )
+        copy.start()
+        y_copies.append(copy)
+    for m in range(nmod):
+        y_copies[m].wait_recv()
+        for k in range(1, ngroup):
+            to = lax.rem(g + k, ngroup)
+            z_send[m, k - 1] = (term(m, to, d) + y_recv[m, to].astype(jnp.float32)).astype(jnp.bfloat16)
+            copy = pltpu.make_async_remote_copy(
+                src_ref=z_send.at[m, k - 1], dst_ref=z_recv.at[m, k - 1],
+                send_sem=z_ss.at[m, k - 1], recv_sem=z_rs.at[m, k - 1],
+                device_id={"group": to}, device_id_type=MESH,
+            )
+            copy.start()
+            z_copies.append(copy)
+        out_ref[m] = term(m, g, d) + y_recv[m, g].astype(jnp.float32)
+    for m in range(nmod):
+        total = out_ref[m]
+        for k in range(1, ngroup):
+            z_copies[m * (ngroup - 1) + k - 1].wait_recv()
+            total = total + z_recv[m, k - 1].astype(jnp.float32)
+        out_ref[m] = total
+    for copy in y_copies + z_copies:
+        copy.wait_send()
+
+
+def kernel_body(mesh, image_feats, image_proj, tokens, counts, pairing, w_up, w_down, w_proj):
+    ngroup, ndp, nmp = mesh.shape["group"], mesh.shape["dp"], mesh.shape["mp"]
+    nr = ngroup * ndp
+    nmod, per, patches, width = tokens.shape
+    hidden, emb = w_up.shape[2], w_proj.shape[2]
+    apd = image_feats.shape[0]
+    sizes = (ngroup, ndp, nmp, per, apd)
+    height = width // nr
+    f32, bf16 = jnp.float32, jnp.bfloat16
+    vmem = pl.BlockSpec(memory_space=pltpu.VMEM)
+    smem = pl.BlockSpec(memory_space=pltpu.SMEM)
+    h, act, token_pool = pl.pallas_call(
+        fwd_kernel,
+        grid=(nmod, per),
+        in_specs=[
+            smem,
+            pl.BlockSpec((1, 1, patches, width), lambda m, s: (m, s, 0, 0)),
+            pl.BlockSpec((1, width, hidden), lambda m, s: (m, 0, 0)),
+        ],
+        out_specs=[
+            pl.BlockSpec((1, width, hidden), lambda m, s: (m * per + s, 0, 0)),
+            pl.BlockSpec((8, hidden), lambda m, s: (0, 0)),
+            pl.BlockSpec((8, width), lambda m, s: (0, 0)),
+        ],
+        out_shape=[
+            jax.ShapeDtypeStruct((nmod * per, width, hidden), bf16),
+            jax.ShapeDtypeStruct((8, hidden), f32),
+            jax.ShapeDtypeStruct((8, width), f32),
+        ],
+        compiler_params=pltpu.CompilerParams(vmem_limit_bytes=40 << 20),
+        name="forward",
+    )(counts, tokens, w_up)
+    image = jnp.pad(image_feats, ((0, 8 - apd), (0, 0)))
+    sem = pltpu.SemaphoreType.DMA
+    d_act, grad_down, grad_proj = pl.pallas_call(
+        functools.partial(mid_kernel, sizes),
+        in_specs=[smem] + [vmem] * 6,
+        out_specs=[vmem] * 3,
+        out_shape=[
+            jax.ShapeDtypeStruct((8, hidden), f32),
+            jax.ShapeDtypeStruct((nmod, height, hidden), f32),
+            jax.ShapeDtypeStruct((nmod, height, emb), f32),
+        ],
+        scratch_shapes=[
+            pltpu.VMEM((nr, 8, emb), f32),
+            pltpu.VMEM((nmp, nr * 8, 128), f32),
+            pltpu.VMEM((nmp, 8, width), f32),
+            pltpu.VMEM((nmp, 8, 128), f32),
+            pltpu.VMEM((nmp, 8, width), f32),
+            pltpu.VMEM((nr, 16, width), bf16),
+            pltpu.VMEM((nr, 16, width), bf16),
+            pltpu.VMEM((width, nr * 16), f32),
+        ]
+        + [sem((nr - 1,))] * 2
+        + [sem((nmp - 1,))] * 8
+        + [sem((nr - 1,))] * 4,
+        compiler_params=pltpu.CompilerParams(
+            collective_id=0, has_side_effects=True, vmem_limit_bytes=40 << 20
+        ),
+        name="middle",
+    )(pairing, image, image_proj, act, token_pool, w_down, w_proj)
+    grad_up = pl.pallas_call(
+        functools.partial(scatter_kernel, sizes),
+        in_specs=[vmem] * 2,
+        out_specs=vmem,
+        out_shape=jax.ShapeDtypeStruct((nmod, height, hidden), f32),
+        scratch_shapes=[
+            pltpu.VMEM((nmod, ngroup, height, hidden), bf16),
+            pltpu.VMEM((nmod, ngroup, height, hidden), bf16),
+            pltpu.VMEM((nmod, ngroup - 1, height, hidden), bf16),
+            pltpu.VMEM((nmod, ngroup - 1, height, hidden), bf16),
+            sem((nmod,)),
+            sem((nmod,)),
+            sem((nmod, ngroup - 1)),
+            sem((nmod, ngroup - 1)),
+        ],
+        compiler_params=pltpu.CompilerParams(
+            collective_id=1, has_side_effects=True, vmem_limit_bytes=40 << 20
+        ),
+        name="scatter",
+    )(h, d_act)
+    return (grad_up, grad_down, grad_proj)
+
 
 def solution(mesh):
     in_specs = (
@@ -151,4 +475,7 @@
         P(None, ("group", "dp"), "mp"),
         P(None, ("group", "dp"), "mp"),
     )
+    devices = mesh.shape["group"] * mesh.shape["dp"]
+    fits = devices <= 8 and mesh.shape["dp"] == 2
+    body = functools.partial(kernel_body, mesh) if fits else plain_body
     return jax.shard_map(body, mesh=mesh, in_specs=in_specs, out_specs=out_specs, check_vma=False)

time: 265 us -> 96.8 us (0.37)
  blocking collectives: 198 us -> 0 us
  Pallas kernels: 0 us -> 89.1 us
  other arithmetic: 21.7 us -> 0 us
  matrix products: 20.9 us -> 0 us
  between operations: 14.4 us -> 0.72 us
  waiting for transfers between devices: 5.06 us -> 0 us
    all_gather x5 -> x0, blocking collectives: 157 us -> none  [the longest x1 32.1 us: body(): lax.all_gather(pool_stack, ('group', 'dp'), axis=1, tiled=True)]
    pallas_call x0 -> x3, Pallas kernels: none -> 89.1 us  [the longest x1 53 us: kernel_body(): pl.pallas_call(functools.partial(scatter_kernel, sizes), in_specs=[vmem]...]
    psum x5 -> x0, blocking collectives: 40.5 us -> none  [the longest x1 12.8 us: body(): pooled = token_pool + lax.psum(jnp.stack(partials), 'mp')]
    dot_general x23 -> x0, matrix products: 20.9 us -> none  [the longest x3 6.47 us: body(): jnp.dot(normed, w_up[modality], preferred_element_type=jnp.float32)]
    reduce_sum x9 -> x0, other arithmetic: 9.77 us -> none  [the longest x3 5.98 us: normalize_rows(): spread = jnp.mean(jnp.square(values - centre), axis=-1, keepdims=True)]
    convert_element_type x7 -> x0, other arithmetic: 7.47 us -> none  [the longest x2 6.45 us: body(): normed = normalize_rows(tokens[modality].astype(jnp.float32))[0].astype(j...]
    reduce_scatter x1 -> x0, waiting for transfers between devices: 5.05 us -> none  [body(): lax.psum_scatter(stacked, ('group', 'dp'), scatter_dimension=1, tiled=True)]
    another operation x3 -> x0, other arithmetic: 3.4 us -> none  [the longest x1 3.37 us: body(): stacked = jnp.stack(joined_list)]
  transfers between devices with their start and end apart: 1 -> 0, of which waited for: 1 -> 0; matrix products, arithmetic and copies ran while one was open for 1% -> 0% of each run, Pallas kernels for 0% -> 0%
where the time goes in v1:
time: 96.8 us; the launch traced here: 96.7 us
  Pallas kernels  89.1 us (92%)
  local copies, waits for them, and re-layouts  6.85 us (7%)
    pallas_call x1, Pallas kernels, kernel_body(): pl.pallas_call(functools.partial(scatter_kernel, sizes), in_specs=[vmem]...  53 us
    pallas_call x1, Pallas kernels, kernel_body(): pl.pallas_call(functools.partial(mid_kernel, sizes), in_specs=[smem] + [v...  28.4 us
    pallas_call x1, Pallas kernels, kernel_body(): pl.pallas_call(fwd_kernel, grid=(nmod, per), in_specs=[smem, pl.BlockSpec...  7.68 us
    unnamed x14, local copies, waits for them, and re-layouts  6.12 us

profile of v1, /device:TPU:0, one launch (start us, length us, event | category | flops | bytes accessed | tf_op | source)
XLA Modules:
  0.0 96.7 jit_solution(14122818205028625879)
XLA Ops:
  0.6 0.0 copy-start
  0.6 0.9 copy.11.counts_ref
  1.6 0.9 copy.13.pair_ref
  2.5 0.7 pad.4.img_ref
  3.2 1.7 %copy.12.tok_ref = bf16[3,2,196,768]{3,2,1,0:T(8,128)(2,1)S(1)} copy(bf16[3,2,196,768]{3,1,2,0:T(2,128)(2,1)} %param.10) | data formatting | bytes 3612672 | tf_op args[2]
  4.9 0.0 copy-done
  4.9 0.0 copy-start.1
  5.0 0.0 copy-start.2
  5.0 0.0 copy-start.3
  5.0 7.7 %forward.1 = (bf16[6,768,768]{2,1,0:T(8,128)(2,1)S(1)}, f32[8,768]{1,0:T(8,128)S(1)}, f32[8,768]{1,0:T(8,128)S(1)}) custom-call(s32[3,2]{1,0:T(4,128)S(1)} %copy.11.counts_ref, bf16[3,2,196,768]{3,2,1,0:T(8,128)(2,1)S(1)} %copy.12.tok_ref, bf16[3,768,768]{2,1,0:T(8,128)(2,1)S(1)} %copy-done), custom_call_target="tpu_custom_call" | custom-call | tf_op jit(solution)/shard_map/forward/pallas_call | solution.py:389
  12.7 0.0 copy-done.1
  12.7 0.0 copy-done.2
  12.7 0.0 copy-done.3
  12.7 28.4 %middle.1 = (f32[8,768]{1,0:T(8,128)S(1)}, f32[3,96,768]{2,1,0:T(8,128)S(1)}, f32[3,96,256]{2,1,0:T(8,128)S(1)}) custom-call(s32[3,2]{1,0:T(4,128)S(1)} %copy.13.pair_ref, bf16[8,1280]{1,0:T(8,128)(2,1)S(1)} %pad.4.img_ref, bf16[1280,256]{1,0:T(8,128)(2,1)S(1)} %copy-done.3, f32[8,768]{1,0:T(8,128)S(1)} %get-tuple-element.10.act_ref, ...), custom_call_target="tpu_custom_call" | custom-call | tf_op jit(solution)/shard_map/middle/pallas_call | solution.py:412
  41.1 53.0 %scatter.1 = f32[3,96,768]{2,1,0:T(8,128)S(1)} custom-call(bf16[6,768,768]{2,1,0:T(8,128)(2,1)S(1)} %get-tuple-element.9.h_ref, f32[8,768]{1,0:T(8,128)S(1)} %get-tuple-element.12.dact_ref), custom_call_target="tpu_custom_call" | custom-call | tf_op jit(solution)/shard_map/scatter/pallas_call | solution.py:439
  94.1 0.9 copy.17
  95.0 0.9 copy.18
  95.9 0.7 copy.19
Async XLA Ops:
  0.6 4.3 %copy-start = (bf16[3,768,768]{2,1,0:T(8,128)(2,1)S(1)}, bf16[3,768,768]{2,1,0:T(8,128)(2,1)}, u32[]{:S(2)}) copy-start(bf16[3,768,768]{2,1,0:T(8,128)(2,1)} %up_ref.1) | copy-start | bytes 10616836
  4.9 7.7 %copy-start.1 = (bf16[3,768,768]{2,1,0:T(8,128)(2,1)S(1)}, bf16[3,768,768]{2,1,0:T(8,128)(2,1)}, u32[]{:S(2)}) copy-start(bf16[3,768,768]{2,1,0:T(8,128)(2,1)} %down_ref.1) | copy-start | bytes 10616836
  5.0 7.7 %copy-start.2 = (bf16[3,768,256]{2,1,0:T(8,128)(2,1)S(1)}, bf16[3,768,256]{2,1,0:T(8,128)(2,1)}, u32[]{:S(2)}) copy-start(bf16[3,768,256]{2,1,0:T(8,128)(2,1)} %proj_ref.1) | copy-start | bytes 3538948
  5.0 7.7 %copy-start.3 = (bf16[1280,256]{1,0:T(8,128)(2,1)S(1)}, bf16[1280,256]{1,0:T(8,128)(2,1)}, u32[]{:S(2)}) copy-start(bf16[1280,256]{1,0:T(8,128)(2,1)} %iproj_ref.1) | copy-start | bytes 1966084

commit v2 on v0

--- a/solution.py
+++ b/solution.py
@@ -1,8 +1,13 @@
+import functools
+
 import jax
 import jax.numpy as jnp
 from jax import lax
+from jax.experimental import pallas as pl
+from jax.experimental.pallas import tpu as pltpu
 from jax.sharding import PartitionSpec as P
 
+MESH = pl.DeviceIdType.MESH
 inverse_temp = 14.285714285714286
 norm_eps = 1e-05
 unit_eps = 1e-06
@@ -28,7 +33,7 @@
     )
 
 
-def body(image_feats, image_proj, tokens, counts, pairing, w_up, w_down, w_proj):
+def plain_body(image_feats, image_proj, tokens, counts, pairing, w_up, w_down, w_proj):
     image_normed = normalize_rows(image_feats.astype(jnp.float32))[0].astype(jnp.bfloat16)
     embed_cols = jnp.dot(image_normed, image_proj, preferred_element_type=jnp.float32)
     anchor_sq = lax.psum(jnp.sum(embed_cols * embed_cols, axis=-1), "mp")
@@ -134,6 +139,313 @@
     stacked = lax.psum_scatter(stacked, ("group", "dp"), scatter_dimension=1, tiled=True)
     return (stacked, down_shards, proj_shards)
 
+def peer_of(r, ndp):
+    return {"group": r // ndp, "dp": lax.rem(r, ndp)}
+
+
+def step_kernel(
+    sizes, count_ref, pair_ref, img_ref, iproj_ref, tok_ref, up_ref, down_ref, proj_ref,
+    gup_ref, gdown_ref, gproj_ref,
+    img, normed_of, sloped_of, h, e_slots, sq_slots, p_slots, l_slots, f_slots, ga, gb, gt,
+    y_send, y_recv, z_send, z_recv,
+    e_ss, e_rs, sq_ss, sq_rs, p_ss, p_rs, l_ss, l_rs, f_ss, f_rs, a_ss, a_rs, b_ss, b_rs,
+    y_ss, y_rs, z_ss, z_rs,
+):
+    ngroup, ndp, nmp, per, apd, cuts = sizes
+    nr = ngroup * ndp
+    g, d = lax.axis_index("group"), lax.axis_index("dp")
+    r = g * ndp + d
+    me = lax.axis_index("mp")
+    nmod = down_ref.shape[0]
+    rows = 8
+    f32, bf16 = jnp.float32, jnp.bfloat16
+    barrier = pltpu.get_barrier_semaphore()
+    for k in range(1, nmp):
+        pl.semaphore_signal(barrier, inc=1, device_id={"mp": lax.rem(me + k, nmp)}, device_id_type=MESH)
+    for k in range(1, nr):
+        pl.semaphore_signal(barrier, inc=1, device_id=peer_of(lax.rem(r + k, nr), ndp), device_id_type=MESH)
+
+    sent = []
+
+    def spread(slots, ss, rs, across_mp, base=0, lead=()):
+        slot = me if across_mp else r
+        out = []
+        for k in range(1, nmp if across_mp else nr):
+            device = {"mp": lax.rem(me + k, nmp)} if across_mp else peer_of(lax.rem(r + k, nr), ndp)
+            ref = slots.at[lead + (slot,)]
+            copy = pltpu.make_async_remote_copy(
+                src_ref=ref, dst_ref=ref, send_sem=ss.at[base + k - 1], recv_sem=rs.at[base + k - 1],
+                device_id=device, device_id_type=MESH,
+            )
+            copy.start()
+            out.append(copy)
+        sent.extend(out)
+        return out
+
+    def arrive(copies):
+        for copy in copies:
+            copy.wait_recv()
+
+    row_id = lax.broadcasted_iota(jnp.int32, (rows, 1), 0)
+    col = lax.broadcasted_iota(jnp.int32, (rows, 128), 1)
+    anchor_of = (col // 8) * apd + col % 8
+    valid = (col % 8 < apd) & (col < nr * 8)
+
+    def matmul(lhs, rhs, left, right):
+        return lax.dot_general(
+            lhs.astype(bf16), rhs, (((left,), (right,)), ((), ())), preferred_element_type=f32
+        )
+
+    act, pool, pooled_copies = [], [], []
+
+    def forward(m):
+        act_rows = jnp.zeros((rows, up_ref.shape[2]), f32)
+        pool_rows = jnp.zeros((rows, tok_ref.shape[3]), f32)
+        for s in range(per):
+            row = m * per + s
+            x = tok_ref[m, s].astype(f32)
+            normed = normalize_rows(x)[0].astype(bf16)
+            normed_of[row] = normed
+            count = jnp.full((x.shape[0], 1), count_ref[m, s], jnp.int32)
+            index = lax.broadcasted_iota(jnp.int32, (x.shape[0], 1), 0)
+            weight = jnp.where(index < count, 1.0 / count.astype(f32), 0.0)
+            pre = jnp.dot(normed, up_ref[m], preferred_element_type=f32)
+            phi = 0.5 * (1.0 + lax.erf(pre * root_half))
+            slope = phi + pre * jnp.exp(-0.5 * pre * pre) * gauss_coef
+            sloped_of[row] = (weight * slope).astype(bf16)
+            here = row_id == row
+            act_rows = jnp.where(here, jnp.sum(weight * (pre * phi), axis=0, keepdims=True), act_rows)
+            pool_rows = jnp.where(here, jnp.sum(weight * x, axis=0, keepdims=True), pool_rows)
+        act_rows = act_rows.astype(bf16).astype(f32)
+        act.append(act_rows)
+        pool.append(pool_rows)
+        p_slots[m, me] = matmul(act_rows, down_ref[m], 1, 1)
+        pooled_copies.append(spread(p_slots, p_ss, p_rs, True, m * (nmp - 1), (m,)))
+
+    feat, scale, embeds, logit_copies = [], [], [], []
+
+    def total_of(slots, m):
+        total = slots[m, 0]
+        for k in range(1, nmp):
+            total = total + slots[m, k]
+        return total
+
+    def score(m, table):
+        arrive(pooled_copies[m])
+        feat_norm, scale_inv = normalize_rows(pool[m] + total_of(p_slots, m))
+        feat.append(feat_norm)
+        scale.append(scale_inv)
+        embedded = matmul(feat_norm, proj_ref[m], 1, 0)
+        embeds.append(embedded)
+        own_sq = jnp.sum(embedded * embedded, axis=-1, keepdims=True)
+        part = matmul(embedded, table, 1, 1)
+        l_slots[m, me] = jnp.where(col < nr * 8, part, own_sq)
+        logit_copies.append(spread(l_slots, l_ss, l_rs, True, m * (nmp - 1), (m,)))
+
+    d_embeds, feat_copies = [], []
+
+    def loss_slope(m, table):
+        hot = jnp.zeros((rows, 128), f32)
+        for s in range(per):
+            hot = jnp.where(valid & (anchor_of == pair_ref[m, s]) & (row_id == m * per + s), 1.0, hot)
+        arrive(logit_copies[m])
+        both = total_of(l_slots, m)
+        inv_norm = lax.rsqrt(both[:, 127:] + unit_eps)
+        logits = jnp.where(valid, inverse_temp * (both * inv_norm), 0.0)
+        expl = jnp.where(valid, jnp.exp(logits), 0.0)
+        prob = (expl / jnp.sum(expl, axis=-1, keepdims=True)).astype(bf16)
+        dots = jnp.sum((prob.astype(f32) - hot) * logits, axis=-1, keepdims=True)
+        d_unit = inverse_temp * (matmul(prob, table, 1, 0) - matmul(hot, table, 1, 0))
+        d_embed = (d_unit - embeds[m] * inv_norm * dots) * inv_norm
+        own = (row_id >= m * per) & (row_id < (m + 1) * per)
+        d_embed = jnp.where(own, d_embed, 0.0).astype(bf16).astype(f32)
+        d_embeds.append(d_embed)
+        f_slots[m, me] = matmul(d_embed, proj_ref[m], 1, 1)
+        feat_copies.append(spread(f_slots, f_ss, f_rs, True, m * (nmp - 1), (m,)))
+
+    def products(m):
+        for s in range(per):
+            row = m * per + s
+            h[row] = lax.dot_general(
+                normed_of[row], sloped_of[row], (((0,), (0,)), ((), ())), preferred_element_type=f32
+            ).astype(bf16)
+
+    d_pools, d_acts, y_copies, z_copies = [], [], [], []
+    height, hidden = gup_ref.shape[1:]
+    width = hidden // cuts
+
+    def term(m, cut, group, dp):
+        at = pl.ds(pl.multiple_of((group * ndp + dp) * height, height), height)
+        total = None
+        for s in range(per):
+            row = m * per + s
+            lanes = slice(cut * width, (cut + 1) * width)
+            part = h[row, at, lanes].astype(f32) * d_acts[m][row : row + 1, lanes]
+            total = part if total is None else total + part
+        return total
+
+    def send_y(m):
+        arrive(feat_copies[m])
+        d_feat = total_of(f_slots, m)
+        d_pooled = scale[m] * (
+            d_feat
+            - jnp.mean(d_feat, axis=-1, keepdims=True)
+            - feat[m] * jnp.mean(d_feat * feat[m], axis=-1, keepdims=True)
+        )
+        d_pools.append(d_pooled)
+        d_acts.append(matmul(d_pooled, down_ref[m], 1, 0))
+        for cut in range(cuts):
+            c = m * cuts + cut
+            for group in range(ngroup):
+                y_send[c, group] = term(m, cut, group, 1 - d).astype(bf16)
+            copy = pltpu.make_async_remote_copy(
+                src_ref=y_send.at[c], dst_ref=y_recv.at[c], send_sem=y_ss.at[c], recv_sem=y_rs.at[c],
+                device_id={"dp": 1 - d}, device_id_type=MESH,
+            )
+            copy.start()
+            y_copies.append(copy)
+
+    def send_z(m):
+        for cut in range(cuts):
+            c = m * cuts + cut
+            y_copies[c].wait_recv()
+            for k in range(1, ngroup):
+                to = lax.rem(g + k, ngroup)
+                z_send[c, k - 1] = (term(m, cut, to, d) + y_recv[c, to].astype(f32)).astype(bf16)
+                copy = pltpu.make_async_remote_copy(
+                    src_ref=z_send.at[c, k - 1], dst_ref=z_recv.at[c, k - 1],
+                    send_sem=z_ss.at[c * (ngroup - 1) + k - 1], recv_sem=z_rs.at[c * (ngroup - 1) + k - 1],
+                    device_id={"group": to}, device_id_type=MESH,
+                )
+                copy.start()
+                z_copies.append(copy)
+            lanes = slice(cut * width, (cut + 1) * width)
+            gup_ref[m, :, lanes] = term(m, cut, g, d) + y_recv[c, g].astype(f32)
+
+    img[...] = jnp.zeros_like(img)
+    img[0:apd, :] = img_ref[...].astype(f32)
+    image = normalize_rows(img[...])[0]
+    e_slots[r] = matmul(image, iproj_ref[...], 1, 0)
+    pl.semaphore_wait(barrier, nmp - 1 + nr - 1)
+    e_copies = spread(e_slots, e_ss, e_rs, False)
+    forward(0)
+    arrive(e_copies)
+    embed = e_slots[...].reshape(nr * 8, -1)
+    square = jnp.sum(embed * embed, axis=-1, keepdims=True)
+    sq_slots[me] = jnp.broadcast_to(square, sq_slots.shape[1:])
+    sq_copies = spread(sq_slots, sq_ss, sq_rs, True)
+    forward(1)
+    arrive(sq_copies)
+    square = sq_slots[0]
+    for k in range(1, nmp):
+        square = square + sq_slots[k]
+    anchors = (embed * lax.rsqrt(square[:, :1] + unit_eps)).astype(bf16)
+    table = jnp.concatenate([anchors, jnp.zeros((128 - nr * 8, anchors.shape[1]), bf16)], axis=0)
+    score(0, table)
+    forward(2)
+    loss_slope(0, table)
+    score(1, table)
+    products(0)
+    send_y(0)
+    score(2, table)
+    ga[r] = jnp.concatenate([act[0] + act[1] + act[2], feat[0] + feat[1] + feat[2]], axis=0).astype(bf16)
+    a_copies = spread(ga, a_ss, a_rs, False)
+    loss_slope(1, table)
+    products(1)
+    loss_slope(2, table)
+    send_y(1)
+    products(2)
+    send_y(2)
+    d_embed = d_embeds[0] + d_embeds[1] + d_embeds[2]
+    wide = jnp.concatenate([d_embed, jnp.zeros((rows, ga.shape[2] - d_embed.shape[1]), f32)], axis=1)
+    gb[r] = jnp.concatenate([d_pools[0] + d_pools[1] + d_pools[2], wide], axis=0).astype(bf16)
+    b_copies = spread(gb, b_ss, b_rs, False)
+    for m in range(nmod):
+        send_z(m)
+
+    arrive(a_copies)
+    arrive(b_copies)
+    all_a = ga[...].reshape(nr * 16, -1)
+    all_b = gb[...].reshape(nr * 16, -1)
+    mine = pl.ds(pl.multiple_of(r * height, height), height)
+    lane = lax.broadcasted_iota(jnp.int32, (1, nr * 16), 1) % 16
+    emb = gproj_ref.shape[2]
+    gt[...] = all_b.astype(f32).T
+    lhs = gt[mine, :]
+    for m in range(nmod):
+        keep = (lane >= m * per) & (lane < (m + 1) * per)
+        gdown_ref[m] = matmul(jnp.where(keep, lhs, 0.0), all_a, 1, 0)
+    gt[...] = all_a.astype(f32).T
+    lhs = gt[mine, :]
+    for m in range(nmod):
+        keep = (lane >= 8 + m * per) & (lane < 8 + (m + 1) * per)
+        gproj_ref[m] = matmul(jnp.where(keep, lhs, 0.0), all_b[:, :emb], 1, 0)
+
+    for m in range(nmod):
+        for cut in range(cuts):
+            c = m * cuts + cut
+            lanes = slice(cut * width, (cut + 1) * width)
+            total = gup_ref[m, :, lanes]
+            for k in range(1, ngroup):
+                z_copies[c * (ngroup - 1) + k - 1].wait_recv()
+                total = total + z_recv[c, k - 1].astype(f32)
+            gup_ref[m, :, lanes] = total
+    for copy in sent + y_copies + z_copies:
+        copy.wait_send()
+
+
+def kernel_body(mesh, image_feats, image_proj, tokens, counts, pairing, w_up, w_down, w_proj):
+    ngroup, ndp, nmp = mesh.shape["group"], mesh.shape["dp"], mesh.shape["mp"]
+    nr = ngroup * ndp
+    nmod, per, patches, width = tokens.shape
+    hidden, emb = w_up.shape[2], w_proj.shape[2]
+    apd, img_width = image_feats.shape
+    cuts = 2
+    sizes = (ngroup, ndp, nmp, per, apd, cuts)
+    height = width // nr
+    f32, bf16 = jnp.float32, jnp.bfloat16
+    vmem = pl.BlockSpec(memory_space=pltpu.VMEM)
+    smem = pl.BlockSpec(memory_space=pltpu.SMEM)
+    sem = pltpu.SemaphoreType.DMA
+    return pl.pallas_call(
+        functools.partial(step_kernel, sizes),
+        in_specs=[smem] * 2 + [vmem] * 6,
+        out_specs=[vmem] * 3,
+        out_shape=[
+            jax.ShapeDtypeStruct((nmod, height, hidden), f32),
+            jax.ShapeDtypeStruct((nmod, height, hidden), f32),
+            jax.ShapeDtypeStruct((nmod, height, emb), f32),
+        ],
+        scratch_shapes=[
+            pltpu.VMEM((8, img_width), f32),
+            pltpu.VMEM((nmod * per, patches, width), bf16),
+            pltpu.VMEM((nmod * per, patches, hidden), bf16),
+            pltpu.VMEM((nmod * per, width, hidden), bf16),
+            pltpu.VMEM((nr, 8, emb), f32),
+            pltpu.VMEM((nmp, nr * 8, 128), f32),
+            pltpu.VMEM((nmod, nmp, 8, width), f32),
+            pltpu.VMEM((nmod, nmp, 8, 128), f32),
+            pltpu.VMEM((nmod, nmp, 8, width), f32),
+            pltpu.VMEM((nr, 16, width), bf16),
+            pltpu.VMEM((nr, 16, width), bf16),
+            pltpu.VMEM((width, nr * 16), f32),
+            pltpu.VMEM((nmod * cuts, ngroup, height, hidden // cuts), bf16),
+            pltpu.VMEM((nmod * cuts, ngroup, height, hidden // cuts), bf16),
+            pltpu.VMEM((nmod * cuts, ngroup - 1, height, hidden // cuts), bf16),
+            pltpu.VMEM((nmod * cuts, ngroup - 1, height, hidden // cuts), bf16),
+        ]
+        + [sem((nr - 1,))] * 2
+        + [sem((nmp - 1,))] * 2
+        + [sem((nmod * (nmp - 1),))] * 6
+        + [sem((nr - 1,))] * 4
+        + [sem((nmod * cuts,))] * 2
+        + [sem((nmod * cuts * (ngroup - 1),))] * 2,
+        compiler_params=pltpu.CompilerParams(
+            collective_id=0, has_side_effects=True, vmem_limit_bytes=44 << 20
+        ),
+        name="step",
+    )(counts, pairing, image_feats, image_proj, tokens, w_up, w_down, w_proj)
+
 
 def solution(mesh):
     in_specs = (
@@ -151,4 +463,7 @@
         P(None, ("group", "dp"), "mp"),
         P(None, ("group", "dp"), "mp"),
     )
+    devices = mesh.shape["group"] * mesh.shape["dp"]
+    fits = devices <= 8 and mesh.shape["dp"] == 2
+    body = functools.partial(kernel_body, mesh) if fits else plain_body
     return jax.shard_map(body, mesh=mesh, in_specs=in_specs, out_specs=out_specs, check_vma=False)

time: 265 us -> 84.5 us (0.32)
  blocking collectives: 198 us -> 0 us
  Pallas kernels: 0 us -> 75.1 us
  other arithmetic: 21.7 us -> 0 us
  matrix products: 20.9 us -> 0 us
  between operations: 14.4 us -> 0.68 us
  waiting for transfers between devices: 5.06 us -> 0 us
  local copies, waits for them, and re-layouts: 4.4 us -> 8.46 us
    all_gather x5 -> x0, blocking collectives: 157 us -> none  [the longest x1 32.1 us: body(): lax.all_gather(pool_stack, ('group', 'dp'), axis=1, tiled=True)]
    pallas_call x0 -> x1, Pallas kernels: none -> 75.1 us  [kernel_body(): pl.pallas_call(functools.partial(step_kernel, sizes), in_specs=[smem] * 2...]
    psum x5 -> x0, blocking collectives: 40.5 us -> none  [the longest x1 12.8 us: body(): pooled = token_pool + lax.psum(jnp.stack(partials), 'mp')]
    dot_general x23 -> x0, matrix products: 20.9 us -> none  [the longest x3 6.47 us: body(): jnp.dot(normed, w_up[modality], preferred_element_type=jnp.float32)]
    reduce_sum x9 -> x0, other arithmetic: 9.77 us -> none  [the longest x3 5.98 us: normalize_rows(): spread = jnp.mean(jnp.square(values - centre), axis=-1, keepdims=True)]
    convert_element_type x7 -> x0, other arithmetic: 7.47 us -> none  [the longest x2 6.45 us: body(): normed = normalize_rows(tokens[modality].astype(jnp.float32))[0].astype(j...]
    unnamed x35 -> x14, local copies, waits for them, and re-layouts: 3.22 us -> 8.46 us
    reduce_scatter x1 -> x0, waiting for transfers between devices: 5.05 us -> none  [body(): lax.psum_scatter(stacked, ('group', 'dp'), scatter_dimension=1, tiled=True)]
  transfers between devices with their start and end apart: 1 -> 0, of which waited for: 1 -> 0; matrix products, arithmetic and copies ran while one was open for 1% -> 0% of each run, Pallas kernels for 0% -> 0%
where the time goes in v2:
time: 84.5 us; the launch traced here: 84.3 us
  Pallas kernels  75.1 us (89%)
  local copies, waits for them, and re-layouts  8.46 us (10%)
    pallas_call x1, Pallas kernels, kernel_body(): pl.pallas_call(functools.partial(step_kernel, sizes), in_specs=[smem] * 2...  75.1 us
    unnamed x14, local copies, waits for them, and re-layouts  8.46 us

profile of v2, /device:TPU:0, one launch (start us, length us, event | category | flops | bytes accessed | tf_op | source)
XLA Modules:
  0.0 84.3 jit_solution(4459594325743973630)
XLA Ops:
  0.6 0.0 copy-start
  0.6 0.9 %copy.11.count_ref = s32[3,2]{1,0:T(4,128)S(1)} copy(s32[3,2]{0,1:T(2,128)} %param.11) | data formatting | bytes 48 | tf_op args[3]
  1.6 0.9 %copy.12.pair_ref = s32[3,2]{1,0:T(4,128)S(1)} copy(s32[3,2]{0,1:T(2,128)} %param.12) | data formatting | bytes 48 | tf_op args[4]
  2.5 0.0 copy-start.3
  2.5 1.7 %copy.13.tok_ref = bf16[3,2,196,768]{3,2,1,0:T(8,128)(2,1)S(1)} copy(bf16[3,2,196,768]{3,1,2,0:T(2,128)(2,1)} %param.10) | data formatting | bytes 3612672 | tf_op args[2]
  4.2 0.0 copy-done
  4.2 0.0 copy-done.3
  4.2 0.0 copy-start.1
  4.2 1.3 %copy-done.1 = bf16[3,768,256]{2,1,0:T(8,128)(2,1)S(1)} copy-done((bf16[3,768,256]{2,1,0:T(8,128)(2,1)S(1)}, bf16[3,768,256]{2,1,0:T(8,128)(2,1)}, u32[]{:S(2)}) %copy-start.1) | copy-done | bytes 1179672
  5.5 0.0 copy-start.2
  5.5 1.1 %copy-done.2 = bf16[1280,256]{1,0:T(8,128)(2,1)S(1)} copy-done((bf16[1280,256]{1,0:T(8,128)(2,1)S(1)}, bf16[1280,256]{1,0:T(8,128)(2,1)}, u32[]{:S(2)}) %copy-start.2) | copy-done | bytes 655384
  6.6 75.1 %step.1 = (f32[3,96,768]{2,1,0:T(8,128)S(1)}, f32[3,96,768]{2,1,0:T(8,128)S(1)}, f32[3,96,256]{2,1,0:T(8,128)S(1)}) custom-call(s32[3,2]{1,0:T(4,128)S(1)} %copy.11.count_ref, s32[3,2]{1,0:T(4,128)S(1)} %copy.12.pair_ref, bf16[6,1280]{1,0:T(8,128)(2,1)S(1)} %copy-done.3, bf16[1280,256]{1,0:T(8,128)(2,1)S(1)} %copy-done.2, ...), custom_call_target="tpu_custom_call" | custom-call | tf_op jit(solution)/shard_map/step/pallas_call | solution.py:410
  81.7 0.9 %copy.17 = f32[3,96,768]{2,1,0:T(8,128)} copy(f32[3,96,768]{2,1,0:T(8,128)S(1)} %get-tuple-element.6) | data formatting | bytes 1769472
  82.6 0.9 %copy.18 = f32[3,96,768]{2,1,0:T(8,128)} copy(f32[3,96,768]{2,1,0:T(8,128)S(1)} %get-tuple-element.7) | data formatting | bytes 1769472
  83.6 0.7 copy.19
Async XLA Ops:
  0.6 3.6 %copy-start = (bf16[3,768,768]{2,1,0:T(8,128)(2,1)S(1)}, bf16[3,768,768]{2,1,0:T(8,128)(2,1)}, u32[]{:S(2)}) copy-start(bf16[3,768,768]{2,1,0:T(8,128)(2,1)} %up_ref.1) | copy-start | bytes 10616836
  2.5 1.7 %copy-start.3 = (bf16[6,1280]{1,0:T(8,128)(2,1)S(1)}, bf16[6,1280]{1,0:T(8,128)(2,1)}, u32[]{:S(2)}) copy-start(bf16[6,1280]{1,0:T(8,128)(2,1)} %img_ref.1) | copy-start | bytes 46084
  4.2 1.3 %copy-start.1 = (bf16[3,768,256]{2,1,0:T(8,128)(2,1)S(1)}, bf16[3,768,256]{2,1,0:T(8,128)(2,1)}, u32[]{:S(2)}) copy-start(bf16[3,768,256]{2,1,0:T(8,128)(2,1)} %proj_ref.1) | copy-start | bytes 3538948
  5.5 1.1 %copy-start.2 = (bf16[1280,256]{1,0:T(8,128)(2,1)S(1)}, bf16[1280,256]{1,0:T(8,128)(2,1)}, u32[]{:S(2)}) copy-start(bf16[1280,256]{1,0:T(8,128)(2,1)} %iproj_ref.1) | copy-start | bytes 1966084

commit v3 on v2

--- a/solution.py
+++ b/solution.py
@@ -144,12 +144,12 @@
 
 
 def step_kernel(
-    sizes, count_ref, pair_ref, img_ref, iproj_ref, tok_ref, up_ref, down_ref, proj_ref,
+    sizes, count_ref, pair_ref, img_ref, iproj_ref, tok_ref, up_hbm, down_hbm, proj_hbm,
     gup_ref, gdown_ref, gproj_ref,
-    img, normed_of, sloped_of, h, e_slots, sq_slots, p_slots, l_slots, f_slots, ga, gb, gt,
-    y_send, y_recv, z_send, z_recv,
+    up_ref, down_ref, proj_ref, w_sem, img, normed_of, sloped_of, h, e_slots, sq_slots, p_slots, l_slots, f_slots, ga, gb, gt,
+    y_send, y_recv, z_send, z_recv, x_send, x_recv,
     e_ss, e_rs, sq_ss, sq_rs, p_ss, p_rs, l_ss, l_rs, f_ss, f_rs, a_ss, a_rs, b_ss, b_rs,
-    y_ss, y_rs, z_ss, z_rs,
+    y_ss, y_rs, z_ss, z_rs, x_ss, x_rs,
 ):
     ngroup, ndp, nmp, per, apd, cuts = sizes
     nr = ngroup * ndp
@@ -159,6 +159,11 @@
     nmod = down_ref.shape[0]
     rows = 8
     f32, bf16 = jnp.float32, jnp.bfloat16
+    loads = {}
+    for m in range(nmod):
+        for i, (src, dst) in enumerate(((up_hbm, up_ref), (down_hbm, down_ref), (proj_hbm, proj_ref))):
+            loads[i, m] = pltpu.make_async_copy(src.at[m], dst.at[m], w_sem.at[i * nmod + m])
+            loads[i, m].start()
     barrier = pltpu.get_barrier_semaphore()
     for k in range(1, nmp):
         pl.semaphore_signal(barrier, inc=1, device_id={"mp": lax.rem(me + k, nmp)}, device_id_type=MESH)
@@ -199,6 +204,7 @@
     act, pool, pooled_copies = [], [], []
 
     def forward(m):
+        loads[0, m].wait()
         act_rows = jnp.zeros((rows, up_ref.shape[2]), f32)
         pool_rows = jnp.zeros((rows, tok_ref.shape[3]), f32)
         for s in range(per):
@@ -206,7 +212,7 @@
             x = tok_ref[m, s].astype(f32)
             normed = normalize_rows(x)[0].astype(bf16)
             normed_of[row] = normed
-            count = jnp.full((x.shape[0], 1), count_ref[m, s], jnp.int32)
+            count = jnp.full((x.shape[0], 1), count_ref[s, m], jnp.int32)
             index = lax.broadcasted_iota(jnp.int32, (x.shape[0], 1), 0)
             weight = jnp.where(index < count, 1.0 / count.astype(f32), 0.0)
             pre = jnp.dot(normed, up_ref[m], preferred_element_type=f32)
@@ -219,6 +225,7 @@
         act_rows = act_rows.astype(bf16).astype(f32)
         act.append(act_rows)
         pool.append(pool_rows)
+        loads[1, m].wait()
         p_slots[m, me] = matmul(act_rows, down_ref[m], 1, 1)
         pooled_copies.append(spread(p_slots, p_ss, p_rs, True, m * (nmp - 1), (m,)))
 
@@ -235,6 +242,7 @@
         feat_norm, scale_inv = normalize_rows(pool[m] + total_of(p_slots, m))
         feat.append(feat_norm)
         scale.append(scale_inv)
+        loads[2, m].wait()
         embedded = matmul(feat_norm, proj_ref[m], 1, 0)
         embeds.append(embedded)
         own_sq = jnp.sum(embedded * embedded, axis=-1, keepdims=True)
@@ -247,7 +255,7 @@
     def loss_slope(m, table):
         hot = jnp.zeros((rows, 128), f32)
         for s in range(per):
-            hot = jnp.where(valid & (anchor_of == pair_ref[m, s]) & (row_id == m * per + s), 1.0, hot)
+            hot = jnp.where(valid & (anchor_of == pair_ref[s, m]) & (row_id == m * per + s), 1.0, hot)
         arrive(logit_copies[m])
         both = total_of(l_slots, m)
         inv_norm = lax.rsqrt(both[:, 127:] + unit_eps)
@@ -270,7 +278,7 @@
                 normed_of[row], sloped_of[row], (((0,), (0,)), ((), ())), preferred_element_type=f32
             ).astype(bf16)
 
-    d_pools, d_acts, y_copies, z_copies = [], [], [], []
+    d_pools, d_acts, y_copies = [], [], []
     height, hidden = gup_ref.shape[1:]
     width = hidden // cuts
 
@@ -305,22 +313,76 @@
             copy.start()
             y_copies.append(copy)
 
-    def send_z(m):
-        for cut in range(cuts):
-            c = m * cuts + cut
-            y_copies[c].wait_recv()
-            for k in range(1, ngroup):
-                to = lax.rem(g + k, ngroup)
-                z_send[c, k - 1] = (term(m, cut, to, d) + y_recv[c, to].astype(f32)).astype(bf16)
-                copy = pltpu.make_async_remote_copy(
-                    src_ref=z_send.at[c, k - 1], dst_ref=z_recv.at[c, k - 1],
-                    send_sem=z_ss.at[c * (ngroup - 1) + k - 1], recv_sem=z_rs.at[c * (ngroup - 1) + k - 1],
-                    device_id={"group": to}, device_id_type=MESH,
-                )
-                copy.start()
-                z_copies.append(copy)
-            lanes = slice(cut * width, (cut + 1) * width)
-            gup_ref[m, :, lanes] = term(m, cut, g, d) + y_recv[c, g].astype(f32)
+    partner = g + 1 - 2 * lax.rem(g, 2)
+    mirror = ngroup - 1 - g
+    mirror_partner = ngroup - 1 - partner
+    is_end = (g == 0) | (g == ngroup - 1)
+    is_middle = jnp.logical_not(is_end)
+    chunks = nmod * cuts
+
+    def z_copy(c, blocks):
+        return pltpu.make_async_remote_copy(
+            src_ref=z_send.at[c, pl.ds(0, blocks)], dst_ref=z_recv.at[c, pl.ds(0, blocks)],
+            send_sem=z_ss.at[c], recv_sem=z_rs.at[c],
+            device_id={"group": partner}, device_id_type=MESH,
+        )
+
+    def x_copy(c, i, to):
+        return pltpu.make_async_remote_copy(
+            src_ref=x_send.at[c, i], dst_ref=x_recv.at[c],
+            send_sem=x_ss.at[2 * c + i], recv_sem=x_rs.at[c],
+            device_id={"group": to}, device_id_type=MESH,
+        )
+
+    def lanes_of(c):
+        return slice((c % cuts) * width, (c % cuts + 1) * width)
+
+    def summed(c, group):
+        return term(c // cuts, c % cuts, group, d) + y_recv[c, group].astype(f32)
+
+    def send_pair(c):
+        y_copies[c].wait_recv()
+        z_send[c, 0] = summed(c, partner).astype(bf16)
+
+        @pl.when(is_end)
+        def _():
+            z_send[c, 1] = summed(c, mirror_partner).astype(bf16)
+            z_send[c, 2] = summed(c, mirror).astype(bf16)
+            z_copy(c, 3).start()
+
+        @pl.when(is_middle)
+        def _():
+            z_copy(c, 1).start()
+
+        gup_ref[c // cuts, :, lanes_of(c)] = summed(c, g)
+
+    def send_across(c):
+        @pl.when(is_middle)
+        def _():
+            z_copy(c, 3).wait_recv()
+            x_send[c, 1] = (summed(c, mirror_partner) + z_recv[c, 2].astype(f32)).astype(bf16)
+            x_copy(c, 1, mirror_partner).start()
+            x_send[c, 0] = (summed(c, mirror) + z_recv[c, 1].astype(f32)).astype(bf16)
+            x_copy(c, 0, mirror).start()
+
+        @pl.when(is_end)
+        def _():
+            z_copy(c, 1).wait_recv()
+
+    def finish(c):
+        x_copy(c, 0, mirror).wait_recv()
+        at = (c // cuts, slice(None), lanes_of(c))
+        gup_ref[at] = gup_ref[at] + z_recv[c, 0].astype(f32) + x_recv[c].astype(f32)
+
+        @pl.when(is_end)
+        def _():
+            z_copy(c, 3).wait_send()
+
+        @pl.when(is_middle)
+        def _():
+            z_copy(c, 1).wait_send()
+            x_copy(c, 0, mirror).wait_send()
+            x_copy(c, 1, mirror_partner).wait_send()
 
     img[...] = jnp.zeros_like(img)
     img[0:apd, :] = img_ref[...].astype(f32)
@@ -354,14 +416,17 @@
     products(1)
     loss_slope(2, table)
     send_y(1)
+    send_pair(0)
     products(2)
     send_y(2)
     d_embed = d_embeds[0] + d_embeds[1] + d_embeds[2]
     wide = jnp.concatenate([d_embed, jnp.zeros((rows, ga.shape[2] - d_embed.shape[1]), f32)], axis=1)
     gb[r] = jnp.concatenate([d_pools[0] + d_pools[1] + d_pools[2], wide], axis=0).astype(bf16)
     b_copies = spread(gb, b_ss, b_rs, False)
-    for m in range(nmod):
-        send_z(m)
+    for c in range(1, chunks):
+        send_pair(c)
+        send_across(c - 1)
+    send_across(chunks - 1)
 
     arrive(a_copies)
     arrive(b_copies)
@@ -381,16 +446,9 @@
         keep = (lane >= 8 + m * per) & (lane < 8 + (m + 1) * per)
         gproj_ref[m] = matmul(jnp.where(keep, lhs, 0.0), all_b[:, :emb], 1, 0)
 
-    for m in range(nmod):
-        for cut in range(cuts):
-            c = m * cuts + cut
-            lanes = slice(cut * width, (cut + 1) * width)
-            total = gup_ref[m, :, lanes]
-            for k in range(1, ngroup):
-                z_copies[c * (ngroup - 1) + k - 1].wait_recv()
-                total = total + z_recv[c, k - 1].astype(f32)
-            gup_ref[m, :, lanes] = total
-    for copy in sent + y_copies + z_copies:
+    for c in range(chunks):
+        finish(c)
+    for copy in sent + y_copies:
         copy.wait_send()
 
 
@@ -409,7 +467,7 @@
     sem = pltpu.SemaphoreType.DMA
     return pl.pallas_call(
         functools.partial(step_kernel, sizes),
-        in_specs=[smem] * 2 + [vmem] * 6,
+        in_specs=[smem] * 2 + [vmem] * 3 + [pl.BlockSpec(memory_space=pl.ANY)] * 3,
         out_specs=[vmem] * 3,
         out_shape=[
             jax.ShapeDtypeStruct((nmod, height, hidden), f32),
@@ -417,6 +475,10 @@
             jax.ShapeDtypeStruct((nmod, height, emb), f32),
         ],
         scratch_shapes=[
+            pltpu.VMEM(w_up.shape, bf16),
+            pltpu.VMEM(w_down.shape, bf16),
+            pltpu.VMEM(w_proj.shape, bf16),
+            sem((3 * nmod,)),
             pltpu.VMEM((8, img_width), f32),
             pltpu.VMEM((nmod * per, patches, width), bf16),
             pltpu.VMEM((nmod * per, patches, hidden), bf16),
@@ -431,20 +493,22 @@
             pltpu.VMEM((width, nr * 16), f32),
             pltpu.VMEM((nmod * cuts, ngroup, height, hidden // cuts), bf16),
             pltpu.VMEM((nmod * cuts, ngroup, height, hidden // cuts), bf16),
-            pltpu.VMEM((nmod * cuts, ngroup - 1, height, hidden // cuts), bf16),
-            pltpu.VMEM((nmod * cuts, ngroup - 1, height, hidden // cuts), bf16),
+            pltpu.VMEM((nmod * cuts, 3, height, hidden // cuts), bf16),
+            pltpu.VMEM((nmod * cuts, 3, height, hidden // cuts), bf16),
+            pltpu.VMEM((nmod * cuts, 2, height, hidden // cuts), bf16),
+            pltpu.VMEM((nmod * cuts, height, hidden // cuts), bf16),
         ]
         + [sem((nr - 1,))] * 2
         + [sem((nmp - 1,))] * 2
         + [sem((nmod * (nmp - 1),))] * 6
         + [sem((nr - 1,))] * 4
-        + [sem((nmod * cuts,))] * 2
-        + [sem((nmod * cuts * (ngroup - 1),))] * 2,
+        + [sem((nmod * cuts,))] * 4
+        + [sem((2 * nmod * cuts,)), sem((nmod * cuts,))],
         compiler_params=pltpu.CompilerParams(
-            collective_id=0, has_side_effects=True, vmem_limit_bytes=44 << 20
+            collective_id=0, has_side_effects=True, vmem_limit_bytes=51 << 20
         ),
         name="step",
-    )(counts, pairing, image_feats, image_proj, tokens, w_up, w_down, w_proj)
+    )(counts.T, pairing.T, image_feats, image_proj, tokens, w_up, w_down, w_proj)
 
 
 def solution(mesh):
@@ -464,6 +528,6 @@
         P(None, ("group", "dp"), "mp"),
     )
     devices = mesh.shape["group"] * mesh.shape["dp"]
-    fits = devices <= 8 and mesh.shape["dp"] == 2
+    fits = devices <= 8 and mesh.shape["dp"] == 2 and mesh.shape["group"] == 4
     body = functools.partial(kernel_body, mesh) if fits else plain_body
     return jax.shard_map(body, mesh=mesh, in_specs=in_specs, out_specs=out_specs, check_vma=False)

time: 84.5 us -> 84.5 us (level)
  Pallas kernels: 75.1 us -> 78.1 us
  local copies, waits for them, and re-layouts: 8.46 us -> 5.6 us
    pallas_call x1, Pallas kernels: 75.1 us -> 78.1 us  [kernel_body(): pl.pallas_call(functools.partial(step_kernel, sizes), in_specs=[smem] * 2...]
    unnamed x14 -> x12, local copies, waits for them, and re-layouts: 8.46 us -> 5.6 us
where the time goes in v3:
time: 84.5 us; the launch traced here: 84.4 us
  Pallas kernels  78.1 us (92%)
  local copies, waits for them, and re-layouts  5.6 us (7%)
    pallas_call x1, Pallas kernels, kernel_body(): pl.pallas_call(functools.partial(step_kernel, sizes), in_specs=[smem] * 2...  78.1 us
    unnamed x12, local copies, waits for them, and re-layouts  5.6 us

profile of v3, /device:TPU:0, one launch (start us, length us, event | category | flops | bytes accessed | tf_op | source)
XLA Modules:
  0.0 84.4 jit_solution(1870804782884170985)
XLA Ops:
  0.6 0.0 copy-start.3
  0.6 0.0 copy-start.2
  0.7 0.0 copy-start
  0.7 0.0 copy-start.1
  0.7 3.0 %copy.11.tok_ref = bf16[3,2,196,768]{3,2,1,0:T(8,128)(2,1)} copy(bf16[3,2,196,768]{3,1,2,0:T(2,128)(2,1)} %param.10) | data formatting | bytes 3612672 | tf_op args[2]
  3.7 0.0 copy-done.3
  3.7 0.0 copy-done.2
  3.7 0.0 copy-done
  3.7 0.0 copy-done.1
  3.7 78.1 %step.1 = (f32[3,96,768]{2,1,0:T(8,128)S(1)}, f32[3,96,768]{2,1,0:T(8,128)S(1)}, f32[3,96,256]{2,1,0:T(8,128)S(1)}) custom-call(s32[2,3]{1,0:T(2,128)S(1)} %bitcast.2, s32[2,3]{1,0:T(2,128)S(1)} %bitcast.3, bf16[6,1280]{1,0:T(8,128)(2,1)S(1)} %copy-done.1, bf16[1280,256]{1,0:T(8,128)(2,1)S(1)} %copy-done, bf16[3,2,196,768]{3,2,1,0:T(8,128)(2,1)} %copy.11.tok_ref, ...), custom_call_target="tpu_custom_call" | custom-call | tf_op jit(solution)/shard_map/step/pallas_call | solution.py:468
  81.8 0.9 %copy.15 = f32[3,96,768]{2,1,0:T(8,128)} copy(f32[3,96,768]{2,1,0:T(8,128)S(1)} %get-tuple-element.6) | data formatting | bytes 1769472
  82.7 0.9 %copy.16 = f32[3,96,768]{2,1,0:T(8,128)} copy(f32[3,96,768]{2,1,0:T(8,128)S(1)} %get-tuple-element.7) | data formatting | bytes 1769472
  83.6 0.7 copy.17
Async XLA Ops:
  0.6 3.1 %copy-start.3 = (s32[3,2]{0,1:T(2,128)S(1)}, s32[3,2]{0,1:T(2,128)}, u32[]{:S(2)}) copy-start(s32[3,2]{0,1:T(2,128)} %param.12) | copy-start | bytes 76
  0.6 3.1 %copy-start.2 = (s32[3,2]{0,1:T(2,128)S(1)}, s32[3,2]{0,1:T(2,128)}, u32[]{:S(2)}) copy-start(s32[3,2]{0,1:T(2,128)} %param.11) | copy-start | bytes 76
  0.7 3.1 %copy-start = (bf16[1280,256]{1,0:T(8,128)(2,1)S(1)}, bf16[1280,256]{1,0:T(8,128)(2,1)}, u32[]{:S(2)}) copy-start(bf16[1280,256]{1,0:T(8,128)(2,1)} %iproj_ref.1) | copy-start | bytes 1966084
  0.7 3.1 %copy-start.1 = (bf16[6,1280]{1,0:T(8,128)(2,1)S(1)}, bf16[6,1280]{1,0:T(8,128)(2,1)}, u32[]{:S(2)}) copy-start(bf16[6,1280]{1,0:T(8,128)(2,1)} %img_ref.1) | copy-start | bytes 46084

commit v4 on v3

--- a/solution.py
+++ b/solution.py
@@ -191,6 +191,28 @@
         for copy in copies:
             copy.wait_recv()
 
+    def gather_y(slots, ss, rs):
+        copy = pltpu.make_async_remote_copy(
+            src_ref=slots.at[r], dst_ref=slots.at[r], send_sem=ss.at[0], recv_sem=rs.at[0],
+            device_id={"dp": 1 - d}, device_id_type=MESH,
+        )
+        copy.start()
+        sent.append(copy)
+        return copy
+
+    def gather_z(slots, ss, rs):
+        out = []
+        ref = slots.at[pl.ds(g * ndp, ndp)]
+        for k in range(1, ngroup):
+            copy = pltpu.make_async_remote_copy(
+                src_ref=ref, dst_ref=ref, send_sem=ss.at[k], recv_sem=rs.at[k],
+                device_id={"group": lax.rem(g + k, ngroup)}, device_id_type=MESH,
+            )
+            copy.start()
+            out.append(copy)
+        sent.extend(out)
+        return out
+
     row_id = lax.broadcasted_iota(jnp.int32, (rows, 1), 0)
     col = lax.broadcasted_iota(jnp.int32, (rows, 128), 1)
     anchor_of = (col // 8) * apd + col % 8
@@ -292,7 +314,7 @@
             total = part if total is None else total + part
         return total
 
-    def send_y(m):
+    def grad_act(m):
         arrive(feat_copies[m])
         d_feat = total_of(f_slots, m)
         d_pooled = scale[m] * (
@@ -302,6 +324,8 @@
         )
         d_pools.append(d_pooled)
         d_acts.append(matmul(d_pooled, down_ref[m], 1, 0))
+
+    def push_y(m):
         for cut in range(cuts):
             c = m * cuts + cut
             for group in range(ngroup):
@@ -408,24 +432,31 @@
     loss_slope(0, table)
     score(1, table)
     products(0)
-    send_y(0)
+    grad_act(0)
+    push_y(0)
     score(2, table)
     ga[r] = jnp.concatenate([act[0] + act[1] + act[2], feat[0] + feat[1] + feat[2]], axis=0).astype(bf16)
-    a_copies = spread(ga, a_ss, a_rs, False)
+    a_first = gather_y(ga, a_ss, a_rs)
     loss_slope(1, table)
     products(1)
     loss_slope(2, table)
-    send_y(1)
+    grad_act(1)
+    push_y(1)
     send_pair(0)
     products(2)
-    send_y(2)
+    grad_act(2)
     d_embed = d_embeds[0] + d_embeds[1] + d_embeds[2]
     wide = jnp.concatenate([d_embed, jnp.zeros((rows, ga.shape[2] - d_embed.shape[1]), f32)], axis=1)
     gb[r] = jnp.concatenate([d_pools[0] + d_pools[1] + d_pools[2], wide], axis=0).astype(bf16)
-    b_copies = spread(gb, b_ss, b_rs, False)
+    b_first = gather_y(gb, b_ss, b_rs)
+    push_y(2)
+    a_first.wait_recv()
+    a_copies = gather_z(ga, a_ss, a_rs)
     for c in range(1, chunks):
         send_pair(c)
         send_across(c - 1)
+    b_first.wait_recv()
+    b_copies = gather_z(gb, b_ss, b_rs)
     send_across(chunks - 1)
 
     arrive(a_copies)
@@ -505,7 +536,7 @@
         + [sem((nmod * cuts,))] * 4
         + [sem((2 * nmod * cuts,)), sem((nmod * cuts,))],
         compiler_params=pltpu.CompilerParams(
-            collective_id=0, has_side_effects=True, vmem_limit_bytes=51 << 20
+            collective_id=0, has_side_effects=True, vmem_limit_bytes=46 << 20
         ),
         name="step",
     )(counts.T, pairing.T, image_feats, image_proj, tokens, w_up, w_down, w_proj)

time: 84.5 us -> 81.6 us (0.966)
  Pallas kernels: 78.1 us -> 76.2 us
  local copies, waits for them, and re-layouts: 5.6 us -> 4.49 us
    pallas_call x1, Pallas kernels: 78.1 us -> 76.2 us  [kernel_body(): pl.pallas_call(functools.partial(step_kernel, sizes), in_specs=[smem] * 2...]
    unnamed x12 -> x14, local copies, waits for them, and re-layouts: 5.6 us -> 4.49 us
where the time goes in v4:
time: 81.6 us; the launch traced here: 81.4 us
  Pallas kernels  76.2 us (93%)
  local copies, waits for them, and re-layouts  4.49 us (6%)
    pallas_call x1, Pallas kernels, kernel_body(): pl.pallas_call(functools.partial(step_kernel, sizes), in_specs=[smem] * 2...  76.2 us
    unnamed x14, local copies, waits for them, and re-layouts  4.49 us

profile of v4, /device:TPU:0, one launch (start us, length us, event | category | flops | bytes accessed | tf_op | source)
XLA Modules:
  0.0 81.4 jit_solution(16220529460849003123)
XLA Ops:
  0.6 0.0 copy-start
  0.6 0.0 copy-start.4
  0.7 0.0 copy-start.3
  0.7 0.0 copy-start.1
  0.7 0.0 copy-start.2
  0.7 1.8 %copy.11.tok_ref = bf16[3,2,196,768]{3,2,1,0:T(8,128)(2,1)S(1)} copy(bf16[3,2,196,768]{3,1,2,0:T(2,128)(2,1)} %param.10) | data formatting | bytes 3612672 | tf_op args[2]
  2.5 0.0 copy-done
  2.5 0.0 copy-done.4
  2.6 0.0 copy-done.3
  2.6 0.1 copy-done.1
  2.7 0.0 copy-done.2
  2.7 76.2 %step.1 = (f32[3,96,768]{2,1,0:T(8,128)S(1)}, f32[3,96,768]{2,1,0:T(8,128)S(1)}, f32[3,96,256]{2,1,0:T(8,128)S(1)}) custom-call(s32[2,3]{1,0:T(2,128)S(1)} %bitcast.2, s32[2,3]{1,0:T(2,128)S(1)} %bitcast.3, bf16[6,1280]{1,0:T(8,128)(2,1)S(1)} %copy-done.2, bf16[1280,256]{1,0:T(8,128)(2,1)S(1)} %copy-done.1, bf16[3,2,196,768]{3,2,1,0:T(8,128)(2,1)S(1)} %copy.11.tok_ref, ...), custom_call_target="tpu_custom_call" | custom-call | tf_op jit(solution)/shard_map/step/pallas_call | solution.py:499
  78.9 0.9 %copy.15 = f32[3,96,768]{2,1,0:T(8,128)} copy(f32[3,96,768]{2,1,0:T(8,128)S(1)} %get-tuple-element.6) | data formatting | bytes 1769472
  79.8 0.9 %copy.16 = f32[3,96,768]{2,1,0:T(8,128)} copy(f32[3,96,768]{2,1,0:T(8,128)S(1)} %get-tuple-element.7) | data formatting | bytes 1769472
  80.7 0.7 copy.17
Async XLA Ops:
  0.6 1.9 %copy-start = (bf16[3,768,256]{2,1,0:T(8,128)(2,1)S(1)}, bf16[3,768,256]{2,1,0:T(8,128)(2,1)}, u32[]{:S(2)}) copy-start(bf16[3,768,256]{2,1,0:T(8,128)(2,1)} %proj_hbm.1) | copy-start | bytes 3538948
  0.6 1.9 %copy-start.4 = (s32[3,2]{0,1:T(2,128)S(1)}, s32[3,2]{0,1:T(2,128)}, u32[]{:S(2)}) copy-start(s32[3,2]{0,1:T(2,128)} %param.12) | copy-start | bytes 76
  0.7 1.9 %copy-start.3 = (s32[3,2]{0,1:T(2,128)S(1)}, s32[3,2]{0,1:T(2,128)}, u32[]{:S(2)}) copy-start(s32[3,2]{0,1:T(2,128)} %param.11) | copy-start | bytes 76
  0.7 2.0 %copy-start.1 = (bf16[1280,256]{1,0:T(8,128)(2,1)S(1)}, bf16[1280,256]{1,0:T(8,128)(2,1)}, u32[]{:S(2)}) copy-start(bf16[1280,256]{1,0:T(8,128)(2,1)} %iproj_ref.1) | copy-start | bytes 1966084
  0.7 2.0 %copy-start.2 = (bf16[6,1280]{1,0:T(8,128)(2,1)S(1)}, bf16[6,1280]{1,0:T(8,128)(2,1)}, u32[]{:S(2)}) copy-start(bf16[6,1280]{1,0:T(8,128)(2,1)} %img_ref.1) | copy-start | bytes 46084
